TPU v7x, 32 devices: a whole 2x2x4 slice. The times are simulated.
32 devices in a mesh: rep: 2 (over x), grp: 16 (over z, y, core).
Axes of the slice: x: 2, y: 2, z: 4, core: 2. Of those that a mesh axis runs over, the one named last changes fastest.
Arguments:
- features: bfloat16 [8192, 128], P('grp'), may hold values from -6 to 6
- weight: bfloat16 [128, 256], replicated, may hold values from -0.5 to 0.5
- bias_row: float32 [256], replicated, may hold values from -3 to 3
- cotangent: bfloat16 [8192, 256], P('grp'), may hold values from -6 to 6
- tile_vals: bfloat16 [2, 16, 8, 12, 128, 128], P('rep', 'grp'), may hold values from -0.1875 to 0.1875
- row_block: int32 [2, 16, 8, 12], P('rep', 'grp'), may hold values from 0 to 3
- col_block: int32 [2, 16, 8, 12], P('rep', 'grp'), may hold values from 0 to 3
- counts: int32 [2, 16, 8], P('rep', 'grp'), may hold values from 1 to 12, as said below
- owner_map: int32 [16], replicated, may hold values from 0 to 15, each once
Outputs:
- hidden: bfloat16 [8192, 256], P('grp')
- grad_w: float32 [128, 256], replicated
- grad_x: float32 [8192, 128], P('grp')
Inputs may be any that keep to these rules, and one draw needn't show every extreme that they name: `counts`: live slots of one device in one section; the most, 12, is reached in every draw. `owner_map`: each index of grp appears once; entries r * 8 to (r + 1) * 8 - 1 are the owners, in section order, whose column blocks replica group r holds.
All inputs are finite; a program needn't handle non-finite values.
Results may differ from a plain program's by a relative error of at most 0.0054.
Values may be sent and summed in bfloat16 or wider, within the bound.
A program may use at most 64 MiB of HBM per device.

v0:
```python
import jax
import jax.numpy as jnp
from jax import lax
from jax.sharding import PartitionSpec as P


def spread(block, axis, source):
    block = jnp.where(lax.axis_index(axis) == source, block, jnp.zeros_like(block))
    return lax.psum(block, axis)


def per_device(
    features, weight, bias_row, cotangent, tile_vals, row_block, col_block, counts, owner_map
):
    tile_set = tile_vals[0, 0]
    row_list = row_block[0, 0]
    col_list = col_block[0, 0]
    count_list = counts[0, 0]
    n_sections = tile_set.shape[0]
    n_slots = tile_set.shape[1]
    tile_side = tile_set.shape[2]
    rows_dev = features.shape[0]
    width_in = features.shape[1]
    n_blocks = rows_dev // tile_side
    replica = lax.axis_index("rep")
    member = lax.axis_index("grp")
    owners = lax.dynamic_slice_in_dim(owner_map, replica * n_sections, n_sections)
    live_slot = jnp.arange(n_slots, dtype=jnp.int32)[None, :] < count_list[:, None]
    block_ids = jnp.arange(n_blocks, dtype=jnp.int32)
    row_pick = (row_list[..., None] == block_ids) & live_slot[..., None]
    col_pick = (col_list[..., None] == block_ids) & live_slot[..., None]
    agg_total = jnp.zeros((n_blocks, tile_side, width_in), jnp.float32)
    for section_idx in range(n_sections):
        remote = spread(features, "grp", owners[section_idx])
        source = jnp.take(
            remote.reshape(n_blocks, tile_side, width_in), col_list[section_idx], axis=0
        )
        product = jnp.einsum(
            "kij,kjd->kid", tile_set[section_idx], source, preferred_element_type=jnp.float32
        )
        agg_total = agg_total + jnp.sum(
            jnp.where(row_pick[section_idx][:, :, None, None], product[:, None], 0.0), axis=0
        )
    mixed_rows = lax.psum(agg_total.reshape(rows_dev, width_in), "rep")
    aggregated = mixed_rows + features.astype(jnp.float32)
    agg_rows = aggregated.astype(jnp.bfloat16)
    pre_act = jnp.dot(agg_rows, weight, preferred_element_type=jnp.float32) + bias_row
    hidden = jax.nn.silu(pre_act).astype(jnp.bfloat16)
    sigmoid_val = jax.nn.sigmoid(pre_act)
    grad_pre = (
        cotangent.astype(jnp.float32) * sigmoid_val * (1.0 + pre_act * (1.0 - sigmoid_val))
    ).astype(jnp.bfloat16)
    weight_term = jnp.dot(agg_rows.T, grad_pre, preferred_element_type=jnp.float32)
    grad_w = lax.psum(weight_term, "grp") * (rows_dev * lax.axis_size("grp")) ** (-0.5)
    back_rows = jnp.dot(grad_pre, weight.T, preferred_element_type=jnp.float32).astype(jnp.bfloat16)
    back_blocks = back_rows.reshape(n_blocks, tile_side, width_in)
    returned = jnp.zeros((rows_dev, width_in), jnp.float32)
    for section_idx in range(n_sections):
        chosen_back = jnp.take(back_blocks, row_list[section_idx], axis=0)
        carried = jnp.einsum(
            "kji,kjd->kid", tile_set[section_idx], chosen_back, preferred_element_type=jnp.float32
        )
        partial_value = jnp.sum(
            jnp.where(col_pick[section_idx][:, :, None, None], carried[:, None], 0.0), axis=0
        ).reshape(rows_dev, width_in)
        summed = lax.psum(partial_value, "grp")
        returned = returned + jnp.where(member == owners[section_idx], summed, 0.0)
    grad_x = lax.psum(returned.astype(jnp.bfloat16), "rep").astype(jnp.float32) + back_rows.astype(
        jnp.float32
    )
    return (hidden, grad_w, grad_x)


def solution(mesh):
    in_specs = (
        P("grp", None),
        P(),
        P(),
        P("grp", None),
        P("rep", "grp", None, None, None, None),
        P("rep", "grp", None, None),
        P("rep", "grp", None, None),
        P("rep", "grp", None),
        P(),
    )
    out_specs = (P("grp", None), P(), P("grp", None))
    return jax.shard_map(
        per_device, mesh=mesh, in_specs=in_specs, out_specs=out_specs, check_vma=False
    )
```

profile of v0, /device:TPU:0, one launch (start us, length us, event | category | flops | bytes accessed | tf_op | source)
XLA Modules:
  0.0 389.1 jit_solution(7909117262598457025)
XLA Ops:
  13.8 1.9 broadcast_select_fusion.6
  15.8 1.6 compare_and_fusion.14
  20.3 1.6 compare_and_fusion.7
  22.0 91.5 %all-reduce.13.cloned.1.call-done = (bf16[4,128,128]{2,1,0:T(8,128)(2,1)}, bf16[4,128,128]{2,1,0:T(8,128)(2,1)}, bf16[4,128,128]{2,1,0:T(8,128)(2,1)}, bf16[4,12...) async-done(((bf16[4,128,128]{2,1,0:T(8,128)(2,1)}, ...) | async-done | bytes 1048592 | tf_op jit(solution)/shard_map/psum | solution.py:9
  113.5 2.3 gather_fusion.7
  115.8 2.5 convolution_bitcast_fusion.8
  118.2 2.3 copy.115
  120.6 1.4 gather_fusion.6
  121.9 2.4 convolution_bitcast_fusion.9
  124.4 2.4 copy.112
  126.7 1.4 gather_fusion.5
  128.1 2.4 convolution_bitcast_fusion.10
  130.6 2.3 copy.109
  132.9 1.4 gather_fusion.4
  134.2 2.4 convolution_bitcast_fusion.11
  136.7 2.3 copy.106
  139.0 1.4 gather_fusion.3
  140.4 2.4 convolution_bitcast_fusion.12
  142.9 2.3 copy.103
  145.2 1.4 gather_fusion.2
  146.6 2.4 convolution_bitcast_fusion.13
  149.0 2.3 copy.100
  151.3 1.4 gather_fusion
  152.7 2.4 convolution_bitcast_fusion.15
  155.1 2.3 copy.94
  157.4 1.4 gather_fusion.1
  158.8 2.5 convolution_bitcast_fusion.14
  161.3 2.3 copy.97
  163.6 1.6 select_reduce_fusion.8
  165.2 1.6 select_reduce_fusion.9
  166.8 1.5 select_reduce_fusion.10
  172.4 21.7 %all-reduce.7.cloned.1.call-done = f32[512,128]{1,0:T(8,128)} async-done(((f32[512,128]{1,0:T(8,128)}), f32[512,128]{1,0:T(8,128)}) %all-reduce.7.cloned.1.call-update) | async-done | bytes 262160 | tf_op jit(solution)/shard_map/psum | solution.py:44
  194.0 2.1 multiply_convert_fusion
  197.1 1.4 gather_fusion.15
  198.5 2.3 convolution_bitcast_fusion
  200.8 2.3 copy.139
  203.1 1.4 gather_fusion.14
  204.4 2.3 convolution_bitcast_fusion.1
  206.7 2.3 copy.136
  209.0 1.4 gather_fusion.13
  210.4 2.3 convolution_bitcast_fusion.2
  212.7 2.3 copy.133
  214.9 1.4 gather_fusion.12
  216.3 2.3 convolution_bitcast_fusion.3
  218.6 2.3 copy.130
  220.9 1.4 gather_fusion.11
  222.3 2.3 convolution_bitcast_fusion.4
  224.6 2.3 copy.127
  226.9 1.4 gather_fusion.10
  228.2 2.3 convolution_bitcast_fusion.5
  230.5 2.3 copy.124
  232.8 1.4 gather_fusion.9
  234.1 2.3 convolution_bitcast_fusion.6
  236.4 2.3 copy.121
  238.7 1.4 gather_fusion.8
  240.1 2.3 convolution_bitcast_fusion.7
  242.4 2.4 copy.118
  244.9 2.3 select_reduce_fusion
  248.3 1.1 select_reduce_fusion.2
  253.5 1.1 select_reduce_fusion.7
  255.6 101.4 %all-reduce.11.cloned.1.call-done = (f32[128,256]{1,0:T(8,128)}, f32[512,128]{1,0:T(8,128)}, f32[512,128]{1,0:T(8,128)}, f32[512,128]{1,0:T(8,128)}, f32[512,128...) async-done(((f32[128,256]{1,0:T(8,128)}, f32[512,128]{1,0:T(8,128)}, f32[512,128]{1,0:T(8,128)}, ...) | async-done | bytes 2228240 | tf_op jit(solution)/shard_map/psum | solution.py:54
  357.8 1.6 broadcast_multiply_fusion
  359.3 21.6 %all-reduce.9.cloned.1.call-done = bf16[512,128]{1,0:T(8,128)(2,1)} async-done(((bf16[512,128]{1,0:T(8,128)(2,1)}), bf16[512,128]{1,0:T(8,128)(2,1)}) %all-reduce.9.cloned.1.call-update) | async-done | bytes 131088 | tf_op jit(solution)/shard_map/psum | solution.py:68
  380.9 1.6 convert_add_fusion
  (149 shorter events, 16.4 us)
Async XLA Ops:
  7.2 186.9 %copy-start = (bf16[128,256]{1,0:T(8,128)(2,1)S(1)}, bf16[128,256]{1,0:T(8,128)(2,1)}, u32[]{:S(2)}) copy-start(bf16[128,256]{1,0:T(8,128)(2,1)} %param.12) | copy-start | bytes 196612
  7.2 108.6 %copy-start.1 = (bf16[1,1,8,12,128,128]{5,4,3,2,1,0:T(8,128)(2,1)S(1)}, bf16[1,1,8,12,128,128]{5,4,3,2,1,0:T(8,128)(2,1)}, u32[]{:S(2)}) copy-start(bf16[1,1,8,12,128,128]{5,4,3,2,1,0:T(8,128)(2,1)} %param.15) | copy-start | bytes 9437188
  7.2 106.3 %all-reduce.13.cloned.1.call-start = ((), (), s32[]{:S(2)}) async-start(), calls=%async_computation.3 | async-start | bytes 2097152 | tf_op jit(solution)/shard_map/psum | solution.py:9
  15.7 178.3 %all-reduce.7.cloned.1.call-start = ((), (), s32[]{:S(2)}) async-start(), calls=%async_computation | async-start | bytes 524288 | tf_op jit(solution)/shard_map/psum | solution.py:44
  113.5 7.1 %copy-start.20 = (bf16[4,128,128]{2,1,0:T(8,128)(2,1)S(1)}, bf16[4,128,128]{2,1,0:T(8,128)(2,1)}, u32[]{:S(2)}) copy-start(bf16[4,128,128]{2,1,0:T(8,128)(2,1)} %get-tuple-element.14) | copy-start | bytes 393220
  118.2 8.5 %copy-start.19 = (bf16[4,128,128]{2,1,0:T(8,128)(2,1)S(1)}, bf16[4,128,128]{2,1,0:T(8,128)(2,1)}, u32[]{:S(2)}) copy-start(bf16[4,128,128]{2,1,0:T(8,128)(2,1)} %get-tuple-element.15) | copy-start | bytes 393220
  124.4 8.5 %copy-start.18 = (bf16[4,128,128]{2,1,0:T(8,128)(2,1)S(1)}, bf16[4,128,128]{2,1,0:T(8,128)(2,1)}, u32[]{:S(2)}) copy-start(bf16[4,128,128]{2,1,0:T(8,128)(2,1)} %get-tuple-element.16) | copy-start | bytes 393220
  124.4 9.9 %copy-start.33 = (pred[12]{0:T(512)(128)(4,1)S(1)}, pred[12]{0:T(512)(128)(4,1)}, u32[]{:S(2)}) copy-start(pred[12]{0:T(512)(128)(4,1)} %get-tuple-element.97) | copy-start | bytes 40
  130.5 8.5 %copy-start.17 = (bf16[4,128,128]{2,1,0:T(8,128)(2,1)S(1)}, bf16[4,128,128]{2,1,0:T(8,128)(2,1)}, u32[]{:S(2)}) copy-start(bf16[4,128,128]{2,1,0:T(8,128)(2,1)} %get-tuple-element.17) | copy-start | bytes 393220
  130.6 9.9 %copy-start.32 = (pred[12]{0:T(512)(128)(4,1)S(1)}, pred[12]{0:T(512)(128)(4,1)}, u32[]{:S(2)}) copy-start(pred[12]{0:T(512)(128)(4,1)} %get-tuple-element.99) | copy-start | bytes 40
  136.7 8.5 %copy-start.16 = (bf16[4,128,128]{2,1,0:T(8,128)(2,1)S(1)}, bf16[4,128,128]{2,1,0:T(8,128)(2,1)}, u32[]{:S(2)}) copy-start(bf16[4,128,128]{2,1,0:T(8,128)(2,1)} %get-tuple-element.18) | copy-start | bytes 393220
  136.7 9.9 %copy-start.31 = (pred[12]{0:T(512)(128)(4,1)S(1)}, pred[12]{0:T(512)(128)(4,1)}, u32[]{:S(2)}) copy-start(pred[12]{0:T(512)(128)(4,1)} %get-tuple-element.101) | copy-start | bytes 40
  142.9 8.5 %copy-start.15 = (bf16[4,128,128]{2,1,0:T(8,128)(2,1)S(1)}, bf16[4,128,128]{2,1,0:T(8,128)(2,1)}, u32[]{:S(2)}) copy-start(bf16[4,128,128]{2,1,0:T(8,128)(2,1)} %get-tuple-element.19) | copy-start | bytes 393220
  142.9 9.8 %copy-start.30 = (pred[12]{0:T(512)(128)(4,1)S(1)}, pred[12]{0:T(512)(128)(4,1)}, u32[]{:S(2)}) copy-start(pred[12]{0:T(512)(128)(4,1)} %get-tuple-element.103) | copy-start | bytes 40
  149.0 8.4 %copy-start.14 = (bf16[4,128,128]{2,1,0:T(8,128)(2,1)S(1)}, bf16[4,128,128]{2,1,0:T(8,128)(2,1)}, u32[]{:S(2)}) copy-start(bf16[4,128,128]{2,1,0:T(8,128)(2,1)} %get-tuple-element.20) | copy-start | bytes 393220
  149.0 9.8 %copy-start.29 = (pred[12]{0:T(512)(128)(4,1)S(1)}, pred[12]{0:T(512)(128)(4,1)}, u32[]{:S(2)}) copy-start(pred[12]{0:T(512)(128)(4,1)} %get-tuple-element.37) | copy-start | bytes 40
  163.6 4.8 %copy-start.3 = (f32[12,128,128]{2,1,0:T(8,128)S(1)}, f32[12,128,128]{2,1,0:T(8,128)}, u32[]{:S(2)}) copy-start(f32[12,128,128]{2,1,0:T(8,128)} %copy.106) | copy-start | bytes 2359300
  163.6 5.1 %copy-start.5 = (f32[12,128,128]{2,1,0:T(8,128)S(1)}, f32[12,128,128]{2,1,0:T(8,128)}, u32[]{:S(2)}) copy-start(f32[12,128,128]{2,1,0:T(8,128)} %copy.103) | copy-start | bytes 2359300
  163.6 5.5 %copy-start.8 = (f32[12,128,128]{2,1,0:T(8,128)S(1)}, f32[12,128,128]{2,1,0:T(8,128)}, u32[]{:S(2)}) copy-start(f32[12,128,128]{2,1,0:T(8,128)} %copy.100) | copy-start | bytes 2359300
  163.6 6.0 %copy-start.10 = (f32[12,128,128]{2,1,0:T(8,128)S(1)}, f32[12,128,128]{2,1,0:T(8,128)}, u32[]{:S(2)}) copy-start(f32[12,128,128]{2,1,0:T(8,128)} %copy.94) | copy-start | bytes 2359300
  165.2 4.7 %copy-start.12 = (f32[12,128,128]{2,1,0:T(8,128)S(1)}, f32[12,128,128]{2,1,0:T(8,128)}, u32[]{:S(2)}) copy-start(f32[12,128,128]{2,1,0:T(8,128)} %copy.97) | copy-start | bytes 2359300
  169.1 2.3 copy-start.46
  169.1 2.3 copy-start.47
  169.1 2.3 copy-start.41
  169.1 2.4 copy-start.40
  169.1 2.5 copy-start.39
  169.1 2.6 copy-start.38
  169.1 2.7 copy-start.37
  169.1 2.8 copy-start.36
  169.1 3.0 copy-start.35
  169.2 3.1 copy-start.34
  169.2 3.2 copy-start.44
  169.2 3.2 copy-start.45
  169.2 3.2 copy-start.42
  169.2 3.2 copy-start.43
  169.2 24.8 %copy-start.23 = (bf16[512,128]{1,0:T(8,128)(2,1)S(1)}, bf16[512,128]{1,0:T(8,128)(2,1)}, u32[]{:S(2)}) copy-start(bf16[512,128]{1,0:T(8,128)(2,1)} %param.11) | copy-start | bytes 393220
  169.2 24.8 %copy-start.48 = (f32[256]{0:T(256)S(1)}, f32[256]{0:T(256)}, u32[]{:S(2)}) copy-start(f32[256]{0:T(256)} %param.13) | copy-start | bytes 3076
  171.1 185.8 %all-reduce.11.cloned.1.call-start = ((), (), s32[]{:S(2)}) async-start(), calls=%async_computation.2 | async-start | bytes 4456448 | tf_op jit(solution)/shard_map/psum | solution.py:54
  196.2 0.7 copy-start.21
  196.2 8.3 %copy-start.28 = (pred[12]{0:T(512)(128)(4,1)S(1)}, pred[12]{0:T(512)(128)(4,1)}, u32[]{:S(2)}) copy-start(pred[12]{0:T(512)(128)(4,1)} %get-tuple-element.83) | copy-start | bytes 40
  200.8 9.6 %copy-start.27 = (pred[12]{0:T(512)(128)(4,1)S(1)}, pred[12]{0:T(512)(128)(4,1)}, u32[]{:S(2)}) copy-start(pred[12]{0:T(512)(128)(4,1)} %get-tuple-element.71) | copy-start | bytes 40
  206.7 9.6 %copy-start.26 = (pred[12]{0:T(512)(128)(4,1)S(1)}, pred[12]{0:T(512)(128)(4,1)}, u32[]{:S(2)}) copy-start(pred[12]{0:T(512)(128)(4,1)} %get-tuple-element.73) | copy-start | bytes 40
  212.7 9.6 %copy-start.25 = (pred[12]{0:T(512)(128)(4,1)S(1)}, pred[12]{0:T(512)(128)(4,1)}, u32[]{:S(2)}) copy-start(pred[12]{0:T(512)(128)(4,1)} %get-tuple-element.75) | copy-start | bytes 40
  242.4 4.8 %copy-start.2 = (f32[12,128,128]{2,1,0:T(8,128)S(1)}, f32[12,128,128]{2,1,0:T(8,128)}, u32[]{:S(2)}) copy-start(f32[12,128,128]{2,1,0:T(8,128)} %copy.136) | copy-start | bytes 2359300
  242.4 5.9 %copy-start.4 = (f32[12,128,128]{2,1,0:T(8,128)S(1)}, f32[12,128,128]{2,1,0:T(8,128)}, u32[]{:S(2)}) copy-start(f32[12,128,128]{2,1,0:T(8,128)} %copy.133) | copy-start | bytes 2359300
  242.4 6.9 %copy-start.6 = (f32[12,128,128]{2,1,0:T(8,128)S(1)}, f32[12,128,128]{2,1,0:T(8,128)}, u32[]{:S(2)}) copy-start(f32[12,128,128]{2,1,0:T(8,128)} %copy.130) | copy-start | bytes 2359300
  242.4 8.0 %copy-start.7 = (f32[12,128,128]{2,1,0:T(8,128)S(1)}, f32[12,128,128]{2,1,0:T(8,128)}, u32[]{:S(2)}) copy-start(f32[12,128,128]{2,1,0:T(8,128)} %copy.127) | copy-start | bytes 2359300
  244.9 6.6 %copy-start.9 = (f32[12,128,128]{2,1,0:T(8,128)S(1)}, f32[12,128,128]{2,1,0:T(8,128)}, u32[]{:S(2)}) copy-start(f32[12,128,128]{2,1,0:T(8,128)} %copy.124) | copy-start | bytes 2359300
  244.9 7.6 %copy-start.11 = (f32[12,128,128]{2,1,0:T(8,128)S(1)}, f32[12,128,128]{2,1,0:T(8,128)}, u32[]{:S(2)}) copy-start(f32[12,128,128]{2,1,0:T(8,128)} %copy.121) | copy-start | bytes 2359300
  247.2 6.3 %copy-start.13 = (f32[12,128,128]{2,1,0:T(8,128)S(1)}, f32[12,128,128]{2,1,0:T(8,128)}, u32[]{:S(2)}) copy-start(f32[12,128,128]{2,1,0:T(8,128)} %copy.118) | copy-start | bytes 2359300
  248.3 6.3 %copy-start.22 = (bf16[512,256]{1,0:T(8,128)(2,1)S(1)}, bf16[512,256]{1,0:T(8,128)(2,1)}, u32[]{:S(2)}) copy-start(bf16[512,256]{1,0:T(8,128)(2,1)} %copy-done.21) | copy-start | bytes 786436
  248.3 6.3 %copy-start.24 = (f32[512,128]{1,0:T(8,128)S(1)}, f32[512,128]{1,0:T(8,128)}, u32[]{:S(2)}) copy-start(f32[512,128]{1,0:T(8,128)} %all-reduce.7.cloned.1.call-done) | copy-start | bytes 786436
  255.5 125.4 %all-reduce.9.cloned.1.call-start = ((), (), s32[]{:S(2)}) async-start(), calls=%async_computation.1 | async-start | bytes 262144 | tf_op jit(solution)/shard_map/psum | solution.py:68
Sparse Core Ops, SparseCore 0:
  15.8 97.5 all-reduce.12
  171.3 22.7 all-reduce.6
  255.6 101.2 all-reduce.10
  359.7 21.1 all-reduce.8
where the time goes:
time: 391 us; the launch traced here: 389 us
  waiting for transfers between devices  236 us (60%)
  local copies, waits for them, and re-layouts  64.7 us (17%)
  matrix products  41.1 us (11%)
  other arithmetic  27.6 us (7%)
  between operations  19.2 us (5%)
    psum x1, waiting for transfers between devices, per_device(): lax.psum(weight_term, 'grp') * (rows_dev * lax.axis_size('grp')) ** (-0.5)  101 us
    psum x1, waiting for transfers between devices, spread(): return lax.psum(block, axis)  91.5 us
    psum x1, waiting for transfers between devices, per_device(): mixed_rows = lax.psum(agg_total.reshape(rows_dev, width_in), 'rep')  21.7 us
    psum x1, waiting for transfers between devices, per_device(): lax.psum(returned.astype(jnp.bfloat16), 'rep').astype(jnp.float32)  21.6 us
    dot_general x8, matrix products, per_device(): jnp.einsum('kij,kjd->kid', tile_set[section_idx], source, preferred_eleme...  19.6 us
    dot_general x8, local copies, waits for them, and re-layouts, per_device(): jnp.einsum('kij,kjd->kid', tile_set[section_idx], source, preferred_eleme...  18.6 us
    dot_general x8, local copies, waits for them, and re-layouts, per_device(): jnp.einsum('kji,kjd->kid', tile_set[section_idx], chosen_back, preferred_...  18.5 us
    dot_general x8, matrix products, per_device(): jnp.einsum('kji,kjd->kid', tile_set[section_idx], chosen_back, preferred_...  18.3 us
  transfers between devices with their start and end apart: 4, of which 4 were waited for; matrix products, arithmetic and copies ran while one was open for 2% of the time, Pallas kernels for 0%

commit v1 on v0

v1 whole, which is shorter than its diff:
```python
import functools

import jax
import jax.numpy as jnp
from jax import lax
from jax.experimental import pallas as pl
from jax.experimental.pallas import tpu as pltpu
from jax.sharding import PartitionSpec as P

BF16 = jnp.bfloat16
F32 = jnp.float32


def build_kernel(row_ref, col_ref, count_ref, tiles_ref, out_ref, acc):
    s = pl.program_id(0)
    side = tiles_ref.shape[-1]
    acc[...] = jnp.zeros_like(acc)

    def add(k, carry):
        rows = pl.ds(pl.multiple_of(row_ref[0, 0, s, k] * side, side), side)
        c = col_ref[0, 0, s, k]
        acc[c, rows, :] += tiles_ref[0, 0, 0, k].astype(F32)
        return carry

    lax.fori_loop(0, count_ref[0, 0, s], add, 0)
    for c in range(acc.shape[0]):
        out_ref[0, :, c * side : (c + 1) * side] = acc[c].astype(BF16)


def build_adjacency(tile_vals, row_block, col_block, counts, n_blocks):
    _, _, n_sections, n_slots, side, _ = tile_vals.shape
    rows = n_blocks * side
    return pl.pallas_call(
        build_kernel,
        out_shape=jax.ShapeDtypeStruct((n_sections, rows, rows), BF16),
        grid_spec=pltpu.PrefetchScalarGridSpec(
            num_scalar_prefetch=3,
            grid=(n_sections,),
            in_specs=[
                pl.BlockSpec((1, 1, 1, n_slots, side, side), lambda s, *_: (0, 0, s, 0, 0, 0))
            ],
            out_specs=pl.BlockSpec((1, rows, rows), lambda s, *_: (s, 0, 0)),
            scratch_shapes=[pltpu.VMEM((n_blocks, rows, side), F32)],
        ),
    )(row_block, col_block, counts, tile_vals)


def main_kernel(
    n_rep, n_z, n_y, n_c, scale,
    owner_ref, feat_ref, weight_ref, bias_ref, cot_ref, adj_ref,
    hidden_ref, gw_ref, gx_ref,
    adj, feats, part, rc, rza, rzb, rya, ryb, xg, xo, gwt, gwc, gwy, gwz, back_ref,
    adj_sem, ag_s, ag_r, sib_s, sib_r, rc_s, rc_r, rs_s, rs_r, x_s, x_r, gw_s, gw_r, gwz_s, gwz_r, gwx_s, gwx_r,
):
    rep = lax.axis_index("rep")
    me = lax.axis_index("grp")
    z = me // (n_y * n_c)
    y = (me // n_c) % n_y
    c = me % n_c
    half = feat_ref.shape[0] // 2
    n_sections = adj_ref.shape[0]
    ROWS_A, ROWS_B = pl.ds(0, half), pl.ds(half, half)

    def dev(zz, yy, cc):
        return (rep, (zz * n_y + yy) * n_c + cc)

    def rcopy(src, dst, s_sem, r_sem, target):
        return pltpu.make_async_remote_copy(
            src_ref=src, dst_ref=dst, send_sem=s_sem, recv_sem=r_sem,
            device_id=target, device_id_type=pl.DeviceIdType.MESH,
        )

    adj_copy = pltpu.make_async_copy(adj_ref, adj.at[pl.ds(0, n_sections)], adj_sem)
    adj_copy.start()

    barrier = pltpu.get_barrier_semaphore()

    def greet(target):
        pl.semaphore_signal(barrier, inc=1, device_id=target, device_id_type=pl.DeviceIdType.MESH)

    greet(dev(z, y, 1 - c))
    greet(dev(z, 1 - y, c))
    for j in range(1, n_z):
        greet(dev((z + j) % n_z, y, c))
    for j in range(1, n_rep):
        greet(((rep + j) % n_rep, me))
    feats[z, y, c] = feat_ref[...]
    adj[n_sections] = jnp.zeros_like(adj[n_sections])
    pl.semaphore_wait(barrier, 2 + n_z - 1 + n_rep - 1)

    def a_z(d, t):
        src = z - t if d == 0 else z + t
        blk = feats.at[src, :, c, ROWS_A]
        return rcopy(blk, blk, ag_s.at[0, d, t], ag_r.at[0, d, t], dev(z + 1 if d == 0 else z - 1, y, c))

    def b_z(d, t):
        src = z - t if d == 0 else z + t
        blk = feats.at[src, y, c, ROWS_B]
        return rcopy(blk, blk, ag_s.at[1, d, t], ag_r.at[1, d, t], dev(z + 1 if d == 0 else z - 1, y, c))

    def send_ok(d, t):
        return (z - t >= 0) & (z + 1 < n_z) if d == 0 else (z + t < n_z) & (z >= 1)

    def recv_ok(d, t):
        return z - 1 - t >= 0 if d == 0 else z + 1 + t < n_z

    def origin(d, t):
        return z - 1 - t if d == 0 else z + 1 + t

    def arrived(kind, d, t):
        src = origin(d, t)
        blk = feats.at[src, :, c, ROWS_A] if kind == 0 else feats.at[src, y, c, ROWS_B]
        if kind == 2:
            blk = feats.at[src, 1 - y, c, ROWS_B]
        return rcopy(blk, blk, ag_s.at[kind, d, t], ag_r.at[kind, d, t], dev(z, y, 1 - c))

    def b_y(d, t):
        src = origin(d, t)
        blk = feats.at[src, y, c, ROWS_B]
        return rcopy(blk, blk, ag_s.at[2, d, t], ag_r.at[2, d, t], dev(z, 1 - y, c))

    def sib(kind, src, i, got=False):
        blk = feats.at[src, :, 1 - c if got else c, ROWS_A if kind == 0 else ROWS_B]
        return rcopy(blk, blk, sib_s.at[kind, i], sib_r.at[kind, i], dev(z, y, 1 - c))

    def own_y(rows, i, got=False):
        blk = feats.at[z, 1 - y if got else y, c, rows]
        return rcopy(blk, blk, ag_s.at[3, i, 0], ag_r.at[3, i, 0], dev(z, 1 - y, c))

    own_y(ROWS_A, 0).start()
    for d in range(2):
        pl.when(send_ok(d, 0))(b_z(d, 0).start)
    own_y(ROWS_B, 1).start()
    own_y(ROWS_A, 0, True).wait_recv()
    for d in range(2):
        pl.when(send_ok(d, 0))(a_z(d, 0).start)
    sib(0, z, 0).start()
    own_y(ROWS_B, 1, True).wait_recv()
    sib(1, z, 0).start()
    for t in range(n_z - 1):
        for d in range(2):
            pl.when(recv_ok(d, t))(arrived(1, d, t).wait_recv)
            if t + 1 < n_z - 1:
                pl.when(send_ok(d, t + 1))(b_z(d, t + 1).start)
            pl.when(recv_ok(d, t))(b_y(d, t).start)
        for d in range(2):
            pl.when(recv_ok(d, t))(arrived(0, d, t).wait_recv)
            if t + 1 < n_z - 1:
                pl.when(send_ok(d, t + 1))(a_z(d, t + 1).start)
            pl.when(recv_ok(d, t))(sib(0, origin(d, t), 1 + 2 * t + d).start)
        for d in range(2):
            pl.when(recv_ok(d, t))(arrived(2, d, t).wait_recv)
            pl.when(recv_ok(d, t))(sib(1, origin(d, t), 1 + 2 * t + d).start)
    for kind in range(2):
        sib(kind, z, 0, True).wait_recv()
    for t in range(n_z - 1):
        for d in range(2):
            for kind in range(2):
                pl.when(recv_ok(d, t))(sib(kind, origin(d, t), 1 + 2 * t + d, True).wait_recv)
    adj_copy.wait()

    def forward(s, total):
        o = owner_ref[rep * n_sections + s]
        f = feats[lax.div(o, n_y * n_c), lax.rem(lax.div(o, n_c), n_y), lax.rem(o, n_c)]
        return total + jnp.dot(adj[s], f, preferred_element_type=F32)

    total = lax.fori_loop(0, n_sections, forward, jnp.zeros(feat_ref.shape, F32))
    xg[rep] = total.astype(BF16)

    def x_copy(buf, kind, j, got=False):
        other = (rep + n_rep - j if got else rep + j) % n_rep
        blk = buf.at[other if got else rep]
        return rcopy(blk, blk, x_s.at[kind, j - 1], x_r.at[kind, j - 1], (other, me))

    for j in range(1, n_rep):
        x_copy(xg, 0, j).start()
    for j in range(1, n_rep):
        x_copy(xg, 0, j, True).wait_recv()
    agg = feat_ref[...].astype(F32)
    for r in range(n_rep):
        agg = agg + xg[r].astype(F32)
    agg_rows = agg.astype(BF16)
    pre = jnp.dot(agg_rows, weight_ref[...], preferred_element_type=F32) + bias_ref[...]
    sig = jax.nn.sigmoid(pre)
    hidden_ref[...] = (pre * sig).astype(BF16)
    grad_pre = (cot_ref[...].astype(F32) * sig * (1.0 + pre * (1.0 - sig))).astype(BF16)
    back = lax.dot_general(
        grad_pre, weight_ref[...], (((1,), (1,)), ((), ())), preferred_element_type=F32
    ).astype(BF16)
    back_ref[...] = back
    gwt[...] = lax.dot_general(agg_rows, grad_pre, (((0,), (0,)), ((), ())), preferred_element_type=F32)

    g_rows = gw_ref.shape[0] // (n_rep * n_c)
    g_cols = gw_ref.shape[1] // n_y

    def g_row(r, cc):
        return pl.ds(pl.multiple_of((r * n_c + cc) * g_rows, g_rows), g_rows)

    def g_col(yy):
        return pl.ds(pl.multiple_of(yy * g_cols, g_cols), g_cols)

    gw_c = rcopy(gwt.at[g_row(rep, 1 - c)], gwc, gw_s.at[0], gw_r.at[0], dev(z, y, 1 - c))
    gw_c.start()

    def rc_copy(d):
        return rcopy(part.at[d, :, 1 - c], rc.at[d], rc_s.at[d], rc_r.at[d], dev(z, y, 1 - c))

    def transposed(d, carry):
        for yy in range(n_y):
            for cc in range(n_c):
                m = (d * n_y + yy) * n_c + cc
                idx = jnp.int32(n_sections)
                for s in range(n_sections):
                    idx = jnp.where(owner_ref[rep * n_sections + s] == m, s, idx)
                part[d, yy, cc] = lax.dot_general(
                    adj[idx], back_ref[...], (((0,), (0,)), ((), ())), preferred_element_type=F32
                ).astype(BF16)
        rc_copy(d).start()
        return carry

    lax.fori_loop(0, n_z, transposed, 0)

    gw_c.wait_recv()
    gwc[...] += gwt[g_row(rep, c), :]
    gw_y = rcopy(gwc.at[:, g_col(1 - y)], gwy, gw_s.at[1], gw_r.at[1], dev(z, 1 - y, c))
    gw_y.start()

    def add_core(d, carry):
        rc_copy(d).wait_recv()
        for yy in range(n_y):
            part[d, yy, c] = (part[d, yy, c].astype(F32) + rc[d, yy].astype(F32)).astype(BF16)
        return carry

    def yb_copy(d):
        return rcopy(part.at[d, 1 - y, c, ROWS_B], ryb.at[d], rs_s.at[3, 0, d], rs_r.at[3, 0, d], dev(z, 1 - y, c))

    def add_core_send(d, carry):
        add_core(d, carry)
        yb_copy(d).start()
        return carry

    lax.fori_loop(0, n_z, add_core_send, 0)

    def rs_dest(d, t):
        return z - n_z + 1 + t if d == 0 else z + n_z - 1 - t

    def rs_send_ok(d, t):
        return z - n_z + 1 + t >= 0 if d == 0 else z + n_z - 1 - t <= n_z - 1

    def rs_send_ok2(d, t):
        dst = rs_dest(d, t)
        return (dst >= 0) & (z >= 1) if d == 0 else (dst <= n_z - 1) & (z <= n_z - 2)

    def rs_recv_ok(d, t):
        w = z + 1 if d == 0 else z - 1
        dst = w - n_z + 1 + t if d == 0 else w + n_z - 1 - t
        return (w <= n_z - 1) & (dst >= 0) if d == 0 else (w >= 0) & (dst <= n_z - 1)

    def rs_recv_dest(d, t):
        return z + 2 - n_z + t if d == 0 else z + n_z - 2 - t

    def za_copy(d, t):
        return rcopy(
            part.at[rs_dest(d, t), :, c, ROWS_A], rza.at[d, t],
            rs_s.at[0, d, t], rs_r.at[0, d, t], dev(z - 1 if d == 0 else z + 1, y, c),
        )

    def zb_copy(d, t):
        return rcopy(
            part.at[rs_dest(d, t), y, c, ROWS_B], rzb.at[d, t],
            rs_s.at[1, d, t], rs_r.at[1, d, t], dev(z - 1 if d == 0 else z + 1, y, c),
        )

    def za_got(d, t):
        return rcopy(
            part.at[z, :, c, ROWS_A], rza.at[d, t],
            rs_s.at[0, d, t], rs_r.at[0, d, t], dev(z, y, 1 - c),
        )

    def zb_got(d, t):
        return rcopy(
            part.at[z, y, c, ROWS_B], rzb.at[d, t],
            rs_s.at[1, d, t], rs_r.at[1, d, t], dev(z, y, 1 - c),
        )

    def take_a(d, t):
        za_got(d, t).wait_recv()
        dst = rs_recv_dest(d, t)
        for yy in range(n_y):
            part[dst, yy, c, ROWS_A] = (
                part[dst, yy, c, ROWS_A].astype(F32) + rza[d, t, yy].astype(F32)
            ).astype(BF16)

    def take_b(d, t):
        zb_got(d, t).wait_recv()
        dst = rs_recv_dest(d, t)
        part[dst, y, c, ROWS_B] = (
            part[dst, y, c, ROWS_B].astype(F32) + rzb[d, t].astype(F32)
        ).astype(BF16)

    for d in range(2):
        pl.when(rs_send_ok2(d, 0))(za_copy(d, 0).start)

    gw_y.wait_recv()
    gwz[z] = gwc[:, g_col(y)] + gwy[...]

    def gz_copy(j, got=False):
        other = (z + n_z - j if got else z + j) % n_z
        blk = gwz.at[other if got else z]
        return rcopy(blk, blk, gwz_s.at[j - 1], gwz_r.at[j - 1], dev(other, y, c))

    for j in range(1, n_z):
        gz_copy(j).start()

    def take_yb(d, carry):
        yb_copy(d).wait_recv()
        part[d, y, c, ROWS_B] = (
            part[d, y, c, ROWS_B].astype(F32) + ryb[d].astype(F32)
        ).astype(BF16)
        return carry

    lax.fori_loop(0, n_z, take_yb, 0)
    for t in range(n_z - 1):
        for d in range(2):
            pl.when(rs_send_ok2(d, t))(zb_copy(d, t).start)
        for d in range(2):
            pl.when(rs_recv_ok(d, t))(functools.partial(take_a, d, t))
            if t + 1 < n_z - 1:
                pl.when(rs_send_ok2(d, t + 1))(za_copy(d, t + 1).start)
        for d in range(2):
            pl.when(rs_recv_ok(d, t))(functools.partial(take_b, d, t))
    ya = rcopy(part.at[z, 1 - y, c, ROWS_A], rya, rs_s.at[2, 0, 0], rs_r.at[2, 0, 0], dev(z, 1 - y, c))
    ya.start()

    for j in range(1, n_z):
        gz_copy(j, True).wait_recv()
    gsum = gwz[0]
    for j in range(1, n_z):
        gsum = gsum + gwz[j]
    gw_ref[g_row(rep, c), g_col(y)] = gsum * scale
    mine = gw_ref.at[g_row(rep, c), g_col(y)]
    g_y = rcopy(mine, mine, gw_s.at[2], gw_r.at[2], dev(z, 1 - y, c))
    g_y.start()

    ya.wait_recv()
    xo[rep, ROWS_B] = part[z, y, c, ROWS_B]
    xo[rep, ROWS_A] = (part[z, y, c, ROWS_A].astype(F32) + rya[...].astype(F32)).astype(BF16)
    for j in range(1, n_rep):
        x_copy(xo, 1, j).start()

    theirs = gw_ref.at[g_row(rep, c), g_col(1 - y)]
    rcopy(theirs, theirs, gw_s.at[2], gw_r.at[2], dev(z, 1 - y, c)).wait_recv()
    strip = gw_ref.at[g_row(rep, c)]
    g_c = rcopy(strip, strip, gw_s.at[3], gw_r.at[3], dev(z, y, 1 - c))
    g_c.start()
    strip2 = gw_ref.at[g_row(rep, 1 - c)]
    rcopy(strip2, strip2, gw_s.at[3], gw_r.at[3], dev(z, y, 1 - c)).wait_recv()

    def gx_copy(j, got=False):
        other = (rep + n_rep - j if got else rep + j) % n_rep
        rows = gw_ref.shape[0] // n_rep
        blk = gw_ref.at[pl.ds(pl.multiple_of((other if got else rep) * rows, rows), rows)]
        return rcopy(blk, blk, gwx_s.at[j - 1], gwx_r.at[j - 1], (other, me))

    for j in range(1, n_rep):
        gx_copy(j).start()
    for j in range(1, n_rep):
        x_copy(xo, 1, j, True).wait_recv()
    out = back_ref[...].astype(F32)
    for r in range(n_rep):
        out = out + xo[r].astype(F32)
    gx_ref[...] = out
    for j in range(1, n_rep):
        gx_copy(j, True).wait_recv()

    own_y(ROWS_A, 0).wait_send()
    own_y(ROWS_B, 1).wait_send()
    for kind in range(2):
        sib(kind, z, 0).wait_send()
    for t in range(n_z - 1):
        for d in range(2):
            pl.when(send_ok(d, t))(a_z(d, t).wait_send)
            pl.when(send_ok(d, t))(b_z(d, t).wait_send)
            pl.when(recv_ok(d, t))(b_y(d, t).wait_send)
            for kind in range(2):
                pl.when(recv_ok(d, t))(sib(kind, origin(d, t), 1 + 2 * t + d).wait_send)
            pl.when(rs_send_ok2(d, t))(za_copy(d, t).wait_send)
            pl.when(rs_send_ok2(d, t))(zb_copy(d, t).wait_send)
    for d in range(n_z):
        rc_copy(d).wait_send()
        yb_copy(d).wait_send()
    ya.wait_send()
    for j in range(1, n_rep):
        x_copy(xg, 0, j).wait_send()
        x_copy(xo, 1, j).wait_send()
        gx_copy(j).wait_send()
    for j in range(1, n_z):
        gz_copy(j).wait_send()
    for g in (gw_c, gw_y, g_y, g_c):
        g.wait_send()


def per_device(
    n_rep, n_grp,
    features, weight, bias_row, cotangent, tile_vals, row_block, col_block, counts, owner_map
):
    side = tile_vals.shape[-1]
    n_sections = tile_vals.shape[2]
    rows, width = features.shape
    hid = weight.shape[1]
    n_c, n_y = 2, 2
    n_z = n_grp // (n_c * n_y)
    half = rows // 2
    adjacency = build_adjacency(tile_vals, row_block, col_block, counts, rows // side)
    vmem = pl.BlockSpec(memory_space=pltpu.VMEM)
    dma = pltpu.SemaphoreType.DMA
    g_rows = width // (n_rep * n_c)
    g_cols = hid // n_y
    return pl.pallas_call(
        functools.partial(main_kernel, n_rep, n_z, n_y, n_c, float((rows * n_grp) ** (-0.5))),
        out_shape=(
            jax.ShapeDtypeStruct((rows, hid), BF16),
            jax.ShapeDtypeStruct((width, hid), F32),
            jax.ShapeDtypeStruct((rows, width), F32),
        ),
        in_specs=[pl.BlockSpec(memory_space=pltpu.SMEM), vmem, vmem, vmem, vmem,
                  pl.BlockSpec(memory_space=pl.ANY)],
        out_specs=(vmem, vmem, vmem),
        scratch_shapes=[
            pltpu.VMEM((n_sections + 1, rows, rows), BF16),
            pltpu.VMEM((n_z, n_y, n_c, rows, width), BF16),
            pltpu.VMEM((n_z, n_y, n_c, rows, width), BF16),
            pltpu.VMEM((n_z, n_y, rows, width), BF16),
            pltpu.VMEM((2, n_z - 1, n_y, half, width), BF16),
            pltpu.VMEM((2, n_z - 1, half, width), BF16),
            pltpu.VMEM((half, width), BF16),
            pltpu.VMEM((n_z, half, width), BF16),
            pltpu.VMEM((n_rep, rows, width), BF16),
            pltpu.VMEM((n_rep, rows, width), BF16),
            pltpu.VMEM((width, hid), F32),
            pltpu.VMEM((g_rows, hid), F32),
            pltpu.VMEM((g_rows, g_cols), F32),
            pltpu.VMEM((n_z, g_rows, g_cols), F32),
            pltpu.VMEM((rows, width), BF16),
            dma,
            dma((4, 2, n_z)), dma((4, 2, n_z)),
            dma((2, 2 * n_z)), dma((2, 2 * n_z)),
            dma((n_z,)), dma((n_z,)),
            dma((4, 2, n_z)), dma((4, 2, n_z)),
            dma((2, n_rep)), dma((2, n_rep)),
            dma((4,)), dma((4,)),
            dma((n_z,)), dma((n_z,)),
            dma((n_rep,)), dma((n_rep,)),
        ],
        compiler_params=pltpu.CompilerParams(
            collective_id=0, has_side_effects=True, vmem_limit_bytes=56 * 1024 * 1024
        ),
    )(owner_map, features, weight, bias_row[None, :], cotangent, adjacency)


def solution(mesh):
    in_specs = (
        P("grp", None),
        P(),
        P(),
        P("grp", None),
        P("rep", "grp", None, None, None, None),
        P("rep", "grp", None, None),
        P("rep", "grp", None, None),
        P("rep", "grp", None),
        P(),
    )
    out_specs = (P("grp", None), P(), P("grp", None))
    return jax.shard_map(
        functools.partial(per_device, mesh.shape["rep"], mesh.shape["grp"]),
        mesh=mesh, in_specs=in_specs, out_specs=out_specs, check_vma=False,
    )
```

time: 391 us -> 78.6 us (0.20)
  waiting for transfers between devices: 236 us -> 0 us
  Pallas kernels: 0 us -> 72.7 us
  local copies, waits for them, and re-layouts: 64.7 us -> 4.91 us
  matrix products: 41.1 us -> 0 us
  other arithmetic: 27.6 us -> 0 us
  between operations: 19.2 us -> 0.64 us
    psum x4 -> x0, waiting for transfers between devices: 236 us -> none  [the longest x1 101 us: per_device(): lax.psum(weight_term, 'grp') * (rows_dev * lax.axis_size('grp')) ** (-0.5)]
    pallas_call x0 -> x2, Pallas kernels: none -> 72.7 us  [the longest x1 65.1 us: per_device(): pl.pallas_call(functools.partial(main_kernel, n_rep, n_z, n_y, n_c, float...]
    dot_general x19 -> x0, matrix products: 41.1 us -> none  [the longest x8 19.6 us: per_device(): jnp.einsum('kij,kjd->kid', tile_set[section_idx], source, preferred_eleme...]
    dot_general x16 -> x0, local copies, waits for them, and re-layouts: 37.1 us -> none  [the longest x8 18.6 us: per_device(): jnp.einsum('kij,kjd->kid', tile_set[section_idx], source, preferred_eleme...]
    gather x16 -> x0, local copies, waits for them, and re-layouts: 22.8 us -> none  [the longest x8 11.9 us: per_device(): jnp.take(remote.reshape(n_blocks, tile_side, width_in), col_list[section_...]
    reduce_sum x16 -> x0, other arithmetic: 16.1 us -> none  [the longest x8 9.69 us: per_device(): jnp.sum(jnp.where(col_pick[section_idx][:, :, None, None], carried[:, Non...]
    unnamed x98 -> x3, local copies, waits for them, and re-layouts: 0.9 us -> 4.91 us
    and x3 -> x0, other arithmetic: 3.92 us -> none  [the longest x1 1.62 us: per_device(): chosen_back = jnp.take(back_blocks, row_list[section_idx], axis=0)]
  transfers between devices with their start and end apart: 4 -> 0, of which waited for: 4 -> 0; matrix products, arithmetic and copies ran while one was open for 2% -> 0% of each run, Pallas kernels for 0% -> 0%
where the time goes in v1:
time: 78.6 us; the launch traced here: 78.2 us
  Pallas kernels  72.7 us (92%)
  local copies, waits for them, and re-layouts  4.91 us (6%)
    pallas_call x1, Pallas kernels, per_device(): pl.pallas_call(functools.partial(main_kernel, n_rep, n_z, n_y, n_c, float...  65.1 us
    pallas_call x1, Pallas kernels, build_adjacency(): pl.pallas_call(build_kernel, out_shape=jax.ShapeDtypeStruct((n_sections,...  7.61 us
    unnamed x3, local copies, waits for them, and re-layouts  4.91 us

profile of v1, /device:TPU:0, one launch (start us, length us, event | category | flops | bytes accessed | tf_op | source)
XLA Modules:
  0.0 78.2 jit_solution(5536722553615750320)
XLA Ops:
  0.6 7.6 %shard_map.112.adj_ref = bf16[8,512,512]{2,1,0:T(8,128)(2,1)} custom-call(s32[1,1,8,12]{3,2,1,0:T(8,128)} %row_ref.1, s32[1,1,8,12]{3,2,1,0:T(8,128)} %col_ref.1, s32[1,1,8]{2,1,0:T(1,128)} %count_ref.1, bf16[1,1,8,12,128,128]{5,4,3,2,1,0:T(8,128)(2,1)} %tiles_ref.1), custom_call_target="tpu_custom_call" | custom-call | tf_op jit(solution)/shard_map/pallas_call | solution.py:33
  8.2 65.1 %shard_map.113 = (bf16[512,256]{1,0:T(8,128)(2,1)}, f32[128,256]{1,0:T(8,128)}, f32[512,128]{1,0:T(8,128)}) custom-call(s32[16]{0:T(128)} %owner_ref.1, bf16[512,128]{1,0:T(8,128)(2,1)} %feat_ref.1, bf16[128,256]{1,0:T(8,128)(2,1)} %weight_ref.1, f32[1,256]{1,0:T(1,128)} %bitcast.1, bf16[512,256]{1,0:T(8,128)(2,1)} %cot_ref.1, ...), custom_call_target="tpu_custom_call" | custom-call | tf_op jit(solution)/shard_map/pallas_call | solution.py:419
  73.3 1.7 %copy.15 = bf16[512,256]{1,0:T(8,128)(2,1)} copy(bf16[512,256]{1,0:T(8,128)(2,1)} %get-tuple-element.6) | data formatting | bytes 524288
  75.0 1.6 %copy.16 = f32[128,256]{1,0:T(8,128)} copy(f32[128,256]{1,0:T(8,128)} %get-tuple-element.7) | data formatting | bytes 262144
  76.6 1.7 %copy.17 = f32[512,128]{1,0:T(8,128)} copy(f32[512,128]{1,0:T(8,128)} %get-tuple-element.8) | data formatting | bytes 524288

commit v2 on v1

--- a/solution.py
+++ b/solution.py
@@ -11,46 +11,12 @@
 F32 = jnp.float32
 
 
-def build_kernel(row_ref, col_ref, count_ref, tiles_ref, out_ref, acc):
-    s = pl.program_id(0)
-    side = tiles_ref.shape[-1]
-    acc[...] = jnp.zeros_like(acc)
-
-    def add(k, carry):
-        rows = pl.ds(pl.multiple_of(row_ref[0, 0, s, k] * side, side), side)
-        c = col_ref[0, 0, s, k]
-        acc[c, rows, :] += tiles_ref[0, 0, 0, k].astype(F32)
-        return carry
-
-    lax.fori_loop(0, count_ref[0, 0, s], add, 0)
-    for c in range(acc.shape[0]):
-        out_ref[0, :, c * side : (c + 1) * side] = acc[c].astype(BF16)
-
-
-def build_adjacency(tile_vals, row_block, col_block, counts, n_blocks):
-    _, _, n_sections, n_slots, side, _ = tile_vals.shape
-    rows = n_blocks * side
-    return pl.pallas_call(
-        build_kernel,
-        out_shape=jax.ShapeDtypeStruct((n_sections, rows, rows), BF16),
-        grid_spec=pltpu.PrefetchScalarGridSpec(
-            num_scalar_prefetch=3,
-            grid=(n_sections,),
-            in_specs=[
-                pl.BlockSpec((1, 1, 1, n_slots, side, side), lambda s, *_: (0, 0, s, 0, 0, 0))
-            ],
-            out_specs=pl.BlockSpec((1, rows, rows), lambda s, *_: (s, 0, 0)),
-            scratch_shapes=[pltpu.VMEM((n_blocks, rows, side), F32)],
-        ),
-    )(row_block, col_block, counts, tile_vals)
-
-
 def main_kernel(
     n_rep, n_z, n_y, n_c, scale,
-    owner_ref, feat_ref, weight_ref, bias_ref, cot_ref, adj_ref,
-    hidden_ref, gw_ref, gx_ref,
-    adj, feats, part, rc, rza, rzb, rya, ryb, xg, xo, gwt, gwc, gwy, gwz, back_ref,
-    adj_sem, ag_s, ag_r, sib_s, sib_r, rc_s, rc_r, rs_s, rs_r, x_s, x_r, gw_s, gw_r, gwz_s, gwz_r, gwx_s, gwx_r,
+    owner_ref, row_ref, col_ref, count_ref, feat_hbm, weight_hbm, bias_ref, cot_hbm, tiles_hbm,
+    hidden_hbm, gw_ref, gx_ref,
+    tiles, feat_ref, weight_ref, cot_ref, hidden_ref, adj, feats, part, rc, rza, rzb, rya, ryb, xg, xo, gwt, gwc, gwy, gwz, back_ref,
+    tile_sem, in_sem, ag_s, ag_r, sib_s, sib_r, rc_s, rc_r, rs_s, rs_r, x_s, x_r, gw_s, gw_r, gwz_s, gwz_r, gwx_s, gwx_r,
 ):
     rep = lax.axis_index("rep")
     me = lax.axis_index("grp")
@@ -58,7 +24,8 @@
     y = (me // n_c) % n_y
     c = me % n_c
     half = feat_ref.shape[0] // 2
-    n_sections = adj_ref.shape[0]
+    n_sections, n_slots, side, _ = tiles.shape
+    n_blocks = feat_ref.shape[0] // side
     ROWS_A, ROWS_B = pl.ds(0, half), pl.ds(half, half)
 
     def dev(zz, yy, cc):
@@ -70,8 +37,13 @@
             device_id=target, device_id_type=pl.DeviceIdType.MESH,
         )
 
-    adj_copy = pltpu.make_async_copy(adj_ref, adj.at[pl.ds(0, n_sections)], adj_sem)
-    adj_copy.start()
+    loads = [
+        pltpu.make_async_copy(feat_hbm, feats.at[z, y, c], in_sem.at[0]),
+        pltpu.make_async_copy(feat_hbm, feat_ref, in_sem.at[1]),
+        pltpu.make_async_copy(weight_hbm, weight_ref, in_sem.at[2]),
+        pltpu.make_async_copy(cot_hbm, cot_ref, in_sem.at[3]),
+    ]
+    loads[0].start()
 
     barrier = pltpu.get_barrier_semaphore()
 
@@ -84,9 +56,50 @@
         greet(dev((z + j) % n_z, y, c))
     for j in range(1, n_rep):
         greet(((rep + j) % n_rep, me))
-    feats[z, y, c] = feat_ref[...]
+    tile_loads = [
+        pltpu.make_async_copy(tiles_hbm.at[0, 0, s], tiles.at[s], tile_sem.at[s])
+        for s in range(n_sections)
+    ]
+    for s in range(n_sections):
+        tile_loads[s].start()
+    for load in loads[1:]:
+        load.start()
     adj[n_sections] = jnp.zeros_like(adj[n_sections])
     pl.semaphore_wait(barrier, 2 + n_z - 1 + n_rep - 1)
+    loads[0].wait()
+
+    part_rows = side // 2
+
+    def build(s):
+        tile_loads[s].wait()
+        place = [
+            jnp.where(
+                k < count_ref[0, 0, s], row_ref[0, 0, s, k] * n_blocks + col_ref[0, 0, s, k], -1
+            )
+            for k in range(n_slots)
+        ]
+
+        def column(j, carry):
+            cols = pl.ds(pl.multiple_of(j * side, side), side)
+            for h in range(2):
+                sums = [jnp.zeros((part_rows, side), F32)] * n_blocks
+                for k in range(n_slots):
+                    tile = tiles[s, k, h * part_rows : (h + 1) * part_rows, :].astype(F32)
+                    for i in range(n_blocks):
+                        pick = jnp.where(place[k] == i * n_blocks + j, 1.0, 0.0).astype(F32)
+                        sums[i] = sums[i] + pick * tile
+                for i in range(n_blocks):
+                    lo = i * side + h * part_rows
+                    adj[s, lo : lo + part_rows, cols] = sums[i].astype(BF16)
+            return carry
+
+        lax.fori_loop(0, n_blocks, column, 0)
+
+    todo = list(range(n_sections))
+
+    def build_next():
+        if todo:
+            build(todo.pop(0))
 
     def a_z(d, t):
         src = z - t if d == 0 else z + t
@@ -131,18 +144,22 @@
     for d in range(2):
         pl.when(send_ok(d, 0))(b_z(d, 0).start)
     own_y(ROWS_B, 1).start()
+    build_next()
     own_y(ROWS_A, 0, True).wait_recv()
     for d in range(2):
         pl.when(send_ok(d, 0))(a_z(d, 0).start)
     sib(0, z, 0).start()
+    build_next()
     own_y(ROWS_B, 1, True).wait_recv()
     sib(1, z, 0).start()
     for t in range(n_z - 1):
+        build_next()
         for d in range(2):
             pl.when(recv_ok(d, t))(arrived(1, d, t).wait_recv)
             if t + 1 < n_z - 1:
                 pl.when(send_ok(d, t + 1))(b_z(d, t + 1).start)
             pl.when(recv_ok(d, t))(b_y(d, t).start)
+        build_next()
         for d in range(2):
             pl.when(recv_ok(d, t))(arrived(0, d, t).wait_recv)
             if t + 1 < n_z - 1:
@@ -151,13 +168,16 @@
         for d in range(2):
             pl.when(recv_ok(d, t))(arrived(2, d, t).wait_recv)
             pl.when(recv_ok(d, t))(sib(1, origin(d, t), 1 + 2 * t + d).start)
+    while todo:
+        build_next()
     for kind in range(2):
         sib(kind, z, 0, True).wait_recv()
     for t in range(n_z - 1):
         for d in range(2):
             for kind in range(2):
                 pl.when(recv_ok(d, t))(sib(kind, origin(d, t), 1 + 2 * t + d, True).wait_recv)
-    adj_copy.wait()
+    for load in loads[1:]:
+        load.wait()
 
     def forward(s, total):
         o = owner_ref[rep * n_sections + s]
@@ -183,6 +203,8 @@
     pre = jnp.dot(agg_rows, weight_ref[...], preferred_element_type=F32) + bias_ref[...]
     sig = jax.nn.sigmoid(pre)
     hidden_ref[...] = (pre * sig).astype(BF16)
+    store = pltpu.make_async_copy(hidden_ref, hidden_hbm, in_sem.at[0])
+    store.start()
     grad_pre = (cot_ref[...].astype(F32) * sig * (1.0 + pre * (1.0 - sig))).astype(BF16)
     back = lax.dot_general(
         grad_pre, weight_ref[...], (((1,), (1,)), ((), ())), preferred_element_type=F32
@@ -329,30 +351,26 @@
                 pl.when(rs_send_ok2(d, t + 1))(za_copy(d, t + 1).start)
         for d in range(2):
             pl.when(rs_recv_ok(d, t))(functools.partial(take_b, d, t))
+        if t == 0:
+            for j in range(1, n_z):
+                gz_copy(j, True).wait_recv()
+            gsum = gwz[0]
+            for j in range(1, n_z):
+                gsum = gsum + gwz[j]
+            gw_ref[g_row(rep, c), g_col(y)] = gsum * scale
+            mine = gw_ref.at[g_row(rep, c), g_col(y)]
+            g_y = rcopy(mine, mine, gw_s.at[2], gw_r.at[2], dev(z, 1 - y, c))
+            g_y.start()
+
+        if t == min(1, n_z - 2):
+            theirs = gw_ref.at[g_row(rep, c), g_col(1 - y)]
+            rcopy(theirs, theirs, gw_s.at[2], gw_r.at[2], dev(z, 1 - y, c)).wait_recv()
+            strip = gw_ref.at[g_row(rep, c)]
+            g_c = rcopy(strip, strip, gw_s.at[3], gw_r.at[3], dev(z, y, 1 - c))
+            g_c.start()
     ya = rcopy(part.at[z, 1 - y, c, ROWS_A], rya, rs_s.at[2, 0, 0], rs_r.at[2, 0, 0], dev(z, 1 - y, c))
     ya.start()
 
-    for j in range(1, n_z):
-        gz_copy(j, True).wait_recv()
-    gsum = gwz[0]
-    for j in range(1, n_z):
-        gsum = gsum + gwz[j]
-    gw_ref[g_row(rep, c), g_col(y)] = gsum * scale
-    mine = gw_ref.at[g_row(rep, c), g_col(y)]
-    g_y = rcopy(mine, mine, gw_s.at[2], gw_r.at[2], dev(z, 1 - y, c))
-    g_y.start()
-
-    ya.wait_recv()
-    xo[rep, ROWS_B] = part[z, y, c, ROWS_B]
-    xo[rep, ROWS_A] = (part[z, y, c, ROWS_A].astype(F32) + rya[...].astype(F32)).astype(BF16)
-    for j in range(1, n_rep):
-        x_copy(xo, 1, j).start()
-
-    theirs = gw_ref.at[g_row(rep, c), g_col(1 - y)]
-    rcopy(theirs, theirs, gw_s.at[2], gw_r.at[2], dev(z, 1 - y, c)).wait_recv()
-    strip = gw_ref.at[g_row(rep, c)]
-    g_c = rcopy(strip, strip, gw_s.at[3], gw_r.at[3], dev(z, y, 1 - c))
-    g_c.start()
     strip2 = gw_ref.at[g_row(rep, 1 - c)]
     rcopy(strip2, strip2, gw_s.at[3], gw_r.at[3], dev(z, y, 1 - c)).wait_recv()
 
@@ -364,6 +382,12 @@
 
     for j in range(1, n_rep):
         gx_copy(j).start()
+    ya.wait_recv()
+    xo[rep, ROWS_B] = part[z, y, c, ROWS_B]
+    xo[rep, ROWS_A] = (part[z, y, c, ROWS_A].astype(F32) + rya[...].astype(F32)).astype(BF16)
+    for j in range(1, n_rep):
+        x_copy(xo, 1, j).start()
+
     for j in range(1, n_rep):
         x_copy(xo, 1, j, True).wait_recv()
     out = back_ref[...].astype(F32)
@@ -373,6 +397,7 @@
     for j in range(1, n_rep):
         gx_copy(j, True).wait_recv()
 
+    store.wait()
     own_y(ROWS_A, 0).wait_send()
     own_y(ROWS_B, 1).wait_send()
     for kind in range(2):
@@ -400,6 +425,11 @@
         g.wait_send()
 
 
+def finish_kernel(a, b, c, a_out, b_out, c_out):
+    for src, dst in ((a, a_out), (b, b_out), (c, c_out)):
+        dst[...] = src[...]
+
+
 def per_device(
     n_rep, n_grp,
     features, weight, bias_row, cotangent, tile_vals, row_block, col_block, counts, owner_map
@@ -411,22 +441,27 @@
     n_c, n_y = 2, 2
     n_z = n_grp // (n_c * n_y)
     half = rows // 2
-    adjacency = build_adjacency(tile_vals, row_block, col_block, counts, rows // side)
     vmem = pl.BlockSpec(memory_space=pltpu.VMEM)
     dma = pltpu.SemaphoreType.DMA
     g_rows = width // (n_rep * n_c)
     g_cols = hid // n_y
-    return pl.pallas_call(
+    smem = pl.BlockSpec(memory_space=pltpu.SMEM)
+    hbm = pl.BlockSpec(memory_space=pl.ANY)
+    outs = pl.pallas_call(
         functools.partial(main_kernel, n_rep, n_z, n_y, n_c, float((rows * n_grp) ** (-0.5))),
         out_shape=(
             jax.ShapeDtypeStruct((rows, hid), BF16),
             jax.ShapeDtypeStruct((width, hid), F32),
             jax.ShapeDtypeStruct((rows, width), F32),
         ),
-        in_specs=[pl.BlockSpec(memory_space=pltpu.SMEM), vmem, vmem, vmem, vmem,
-                  pl.BlockSpec(memory_space=pl.ANY)],
-        out_specs=(vmem, vmem, vmem),
+        in_specs=[smem, smem, smem, smem, hbm, hbm, vmem, hbm, hbm],
+        out_specs=(hbm, vmem, vmem),
         scratch_shapes=[
+            pltpu.VMEM(tile_vals.shape[2:], BF16),
+            pltpu.VMEM((rows, width), BF16),
+            pltpu.VMEM((width, hid), BF16),
+            pltpu.VMEM((rows, hid), BF16),
+            pltpu.VMEM((rows, hid), BF16),
             pltpu.VMEM((n_sections + 1, rows, rows), BF16),
             pltpu.VMEM((n_z, n_y, n_c, rows, width), BF16),
             pltpu.VMEM((n_z, n_y, n_c, rows, width), BF16),
@@ -442,7 +477,7 @@
             pltpu.VMEM((g_rows, g_cols), F32),
             pltpu.VMEM((n_z, g_rows, g_cols), F32),
             pltpu.VMEM((rows, width), BF16),
-            dma,
+            dma((n_sections,)), dma((4,)),
             dma((4, 2, n_z)), dma((4, 2, n_z)),
             dma((2, 2 * n_z)), dma((2, 2 * n_z)),
             dma((n_z,)), dma((n_z,)),
@@ -455,7 +490,13 @@
         compiler_params=pltpu.CompilerParams(
             collective_id=0, has_side_effects=True, vmem_limit_bytes=56 * 1024 * 1024
         ),
-    )(owner_map, features, weight, bias_row[None, :], cotangent, adjacency)
+    )(owner_map, row_block, col_block, counts, features, weight, bias_row[None, :], cotangent, tile_vals)
+    return pl.pallas_call(
+        finish_kernel,
+        out_shape=tuple(jax.ShapeDtypeStruct(o.shape, o.dtype) for o in outs),
+        in_specs=[vmem] * 3,
+        out_specs=(vmem,) * 3,
+    )(*outs)
 
 
 def solution(mesh):

time: 78.6 us -> 67.3 us (0.86)
  Pallas kernels: 72.7 us -> 66.5 us
  local copies, waits for them, and re-layouts: 4.91 us -> 0 us
    pallas_call x1, Pallas kernels: 7.61 us -> 1.94 us  [per_device(): pl.pallas_call(finish_kernel, out_shape=tuple((jax.ShapeDtypeStruct(o.sha...]
    unnamed x3 -> x0, local copies, waits for them, and re-layouts: 4.91 us -> none
where the time goes in v2:
time: 67.3 us; the launch traced here: 67.2 us
  Pallas kernels  66.5 us (99%)
    pallas_call x1, Pallas kernels, per_device(): pl.pallas_call(functools.partial(main_kernel, n_rep, n_z, n_y, n_c, float...  64.6 us
    pallas_call x1, Pallas kernels, per_device(): pl.pallas_call(finish_kernel, out_shape=tuple((jax.ShapeDtypeStruct(o.sha...  1.94 us

profile of v2, /device:TPU:0, one launch (start us, length us, event | category | flops | bytes accessed | tf_op | source)
XLA Modules:
  0.0 67.2 jit_solution(16891270075401914069)
XLA Ops:
  0.6 64.6 %shard_map.112 = (bf16[512,256]{1,0:T(8,128)(2,1)}, f32[128,256]{1,0:T(8,128)}, f32[512,128]{1,0:T(8,128)}) custom-call(s32[16]{0:T(128)} %owner_ref.1, s32[1,1,8,12]{3,2,1,0:T(8,128)} %row_ref.1, s32[1,1,8,12]{3,2,1,0:T(8,128)} %col_ref.1, s32[1,1,8]{2,1,0:T(1,128)} %count_ref.1, bf16[512,128]{1,0:T(8,128)(2,1)} %feat_hbm.1, bf16[128,256]{1,0:T(8,128)(2,1)} %weight_hbm.1, ...), custom_call_target="tpu_custom_call" | custom-call | tf_op jit(solution)/shard_map/pallas_call | solution.py:450
  65.2 1.9 %shard_map.113 = (bf16[512,256]{1,0:T(8,128)(2,1)}, f32[128,256]{1,0:T(8,128)}, f32[512,128]{1,0:T(8,128)}) custom-call(bf16[512,256]{1,0:T(8,128)(2,1)} %get-tuple-element.6.a, f32[128,256]{1,0:T(8,128)} %get-tuple-element.7.b, f32[512,128]{1,0:T(8,128)} %get-tuple-element.8.c), custom_call_target="tpu_custom_call" | custom-call | tf_op jit(solution)/shard_map/pallas_call | solution.py:494

commit v3 on v2

--- a/solution.py
+++ b/solution.py
@@ -23,10 +23,11 @@
     z = me // (n_y * n_c)
     y = (me // n_c) % n_y
     c = me % n_c
-    half = feat_ref.shape[0] // 2
+    cut = rya.shape[0]
+    short = n_z == 4
     n_sections, n_slots, side, _ = tiles.shape
     n_blocks = feat_ref.shape[0] // side
-    ROWS_A, ROWS_B = pl.ds(0, half), pl.ds(half, half)
+    ROWS_A, ROWS_B = pl.ds(0, cut), pl.ds(cut, feat_ref.shape[0] - cut)
 
     def dev(zz, yy, cc):
         return (rep, (zz * n_y + yy) * n_c + cc)
@@ -101,17 +102,24 @@
         if todo:
             build(todo.pop(0))
 
-    def a_z(d, t):
-        src = z - t if d == 0 else z + t
+    def a_z(d, t, jump=False):
+        src = z if jump else z - t if d == 0 else z + t
         blk = feats.at[src, :, c, ROWS_A]
-        return rcopy(blk, blk, ag_s.at[0, d, t], ag_r.at[0, d, t], dev(z + 1 if d == 0 else z - 1, y, c))
-
-    def b_z(d, t):
-        src = z - t if d == 0 else z + t
+        step = 2 if jump else 1
+        return rcopy(blk, blk, ag_s.at[0, d, t], ag_r.at[0, d, t], dev(z + step if d == 0 else z - step, y, c))
+
+    def b_z(d, t, jump=False):
+        src = z if jump else z - t if d == 0 else z + t
         blk = feats.at[src, y, c, ROWS_B]
-        return rcopy(blk, blk, ag_s.at[1, d, t], ag_r.at[1, d, t], dev(z + 1 if d == 0 else z - 1, y, c))
+        step = 2 if jump else 1
+        return rcopy(blk, blk, ag_s.at[1, d, t], ag_r.at[1, d, t], dev(z + step if d == 0 else z - step, y, c))
+
+    def jump_ok(d):
+        return z == 0 if d == 0 else z == n_z - 1
 
     def send_ok(d, t):
+        if short and t == 1:
+            return z == 2 if d == 0 else z == 1
         return (z - t >= 0) & (z + 1 < n_z) if d == 0 else (z + t < n_z) & (z >= 1)
 
     def recv_ok(d, t):
@@ -143,11 +151,15 @@
     own_y(ROWS_A, 0).start()
     for d in range(2):
         pl.when(send_ok(d, 0))(b_z(d, 0).start)
+        if short:
+            pl.when(jump_ok(d))(b_z(d, 1, True).start)
     own_y(ROWS_B, 1).start()
     build_next()
     own_y(ROWS_A, 0, True).wait_recv()
     for d in range(2):
         pl.when(send_ok(d, 0))(a_z(d, 0).start)
+        if short:
+            pl.when(jump_ok(d))(a_z(d, 1, True).start)
     sib(0, z, 0).start()
     build_next()
     own_y(ROWS_B, 1, True).wait_recv()
@@ -190,6 +202,11 @@
     def x_copy(buf, kind, j, got=False):
         other = (rep + n_rep - j if got else rep + j) % n_rep
         blk = buf.at[other if got else rep]
+        return rcopy(blk, blk, x_s.at[kind, j - 1], x_r.at[kind, j - 1], (other, me))
+
+    def xo_copy(j, rows, kind, got=False):
+        other = (rep + n_rep - j if got else rep + j) % n_rep
+        blk = xo.at[other if got else rep, rows]
         return rcopy(blk, blk, x_s.at[kind, j - 1], x_r.at[kind, j - 1], (other, me))
 
     for j in range(1, n_rep):
@@ -256,41 +273,50 @@
     def yb_copy(d):
         return rcopy(part.at[d, 1 - y, c, ROWS_B], ryb.at[d], rs_s.at[3, 0, d], rs_r.at[3, 0, d], dev(z, 1 - y, c))
 
-    def add_core_send(d, carry):
-        add_core(d, carry)
-        yb_copy(d).start()
-        return carry
-
-    lax.fori_loop(0, n_z, add_core_send, 0)
-
     def rs_dest(d, t):
         return z - n_z + 1 + t if d == 0 else z + n_z - 1 - t
-
-    def rs_send_ok(d, t):
-        return z - n_z + 1 + t >= 0 if d == 0 else z + n_z - 1 - t <= n_z - 1
 
     def rs_send_ok2(d, t):
         dst = rs_dest(d, t)
         return (dst >= 0) & (z >= 1) if d == 0 else (dst <= n_z - 1) & (z <= n_z - 2)
 
+    def at_end(d):
+        return z == n_z - 1 if d == 0 else z == 0
+
+    def at_second(d):
+        return z == n_z - 2 if d == 0 else z == 1
+
+    def at_third(d):
+        return z == 1 if d == 0 else z == n_z - 2
+
+    def at_far(d):
+        return z == 0 if d == 0 else z == n_z - 1
+
+    def rs_target(d, t):
+        step = jnp.where(at_second(d), 2, 1) if short and t == 1 else 1
+        return dev(z - step if d == 0 else z + step, y, c)
+
     def rs_recv_ok(d, t):
+        if short and t == 1:
+            return at_second(d) | at_far(d)
         w = z + 1 if d == 0 else z - 1
         dst = w - n_z + 1 + t if d == 0 else w + n_z - 1 - t
         return (w <= n_z - 1) & (dst >= 0) if d == 0 else (w >= 0) & (dst <= n_z - 1)
 
     def rs_recv_dest(d, t):
-        return z + 2 - n_z + t if d == 0 else z + n_z - 2 - t
+        dst = z + 2 - n_z + t if d == 0 else z + n_z - 2 - t
+        return jnp.where(at_far(d), z, dst) if short and t == 1 else dst
 
     def za_copy(d, t):
         return rcopy(
             part.at[rs_dest(d, t), :, c, ROWS_A], rza.at[d, t],
-            rs_s.at[0, d, t], rs_r.at[0, d, t], dev(z - 1 if d == 0 else z + 1, y, c),
+            rs_s.at[0, d, t], rs_r.at[0, d, t], rs_target(d, t),
         )
 
     def zb_copy(d, t):
         return rcopy(
             part.at[rs_dest(d, t), y, c, ROWS_B], rzb.at[d, t],
-            rs_s.at[1, d, t], rs_r.at[1, d, t], dev(z - 1 if d == 0 else z + 1, y, c),
+            rs_s.at[1, d, t], rs_r.at[1, d, t], rs_target(d, t),
         )
 
     def za_got(d, t):
@@ -320,8 +346,21 @@
             part[dst, y, c, ROWS_B].astype(F32) + rzb[d, t].astype(F32)
         ).astype(BF16)
 
-    for d in range(2):
-        pl.when(rs_send_ok2(d, 0))(za_copy(d, 0).start)
+    def first_sends(copy_of, dst):
+        for d in range(2):
+            t = dst if d == 0 else n_z - 1 - dst
+            if t < n_z - 1 and (short or t == 0):
+                pl.when(at_end(d))(copy_of(d, t).start)
+            if short and t == 0:
+                pl.when(at_third(d))(copy_of(d, n_z - 2).start)
+
+    def later_send(copy_of, d, t):
+        pl.when(at_second(d) if short else rs_send_ok2(d, t))(copy_of(d, t).start)
+
+    for dst in range(n_z):
+        add_core(dst, 0)
+        yb_copy(dst).start()
+        first_sends(za_copy, dst)
 
     gw_y.wait_recv()
     gwz[z] = gwc[:, g_col(y)] + gwy[...]
@@ -341,17 +380,23 @@
         ).astype(BF16)
         return carry
 
-    lax.fori_loop(0, n_z, take_yb, 0)
-    for t in range(n_z - 1):
-        for d in range(2):
-            pl.when(rs_send_ok2(d, t))(zb_copy(d, t).start)
-        for d in range(2):
-            pl.when(rs_recv_ok(d, t))(functools.partial(take_a, d, t))
+    def take_all(take, copy_of, t):
+        for d in range(2):
+            pl.when(rs_recv_ok(d, t))(functools.partial(take, d, t))
             if t + 1 < n_z - 1:
-                pl.when(rs_send_ok2(d, t + 1))(za_copy(d, t + 1).start)
-        for d in range(2):
-            pl.when(rs_recv_ok(d, t))(functools.partial(take_b, d, t))
-        if t == 0:
+                later_send(copy_of, d, t + 1)
+
+    take_all(take_a, za_copy, 0)
+    for dst in range(n_z):
+        take_yb(dst, 0)
+        first_sends(zb_copy, dst)
+    for t in range(1, n_z - 1):
+        take_all(take_a, za_copy, t)
+        if t == n_z - 2:
+            ya = rcopy(part.at[z, 1 - y, c, ROWS_A], rya, rs_s.at[2, 0, 0], rs_r.at[2, 0, 0], dev(z, 1 - y, c))
+            ya.start()
+        take_all(take_b, zb_copy, t - 1)
+        if t == 1:
             for j in range(1, n_z):
                 gz_copy(j, True).wait_recv()
             gsum = gwz[0]
@@ -362,14 +407,15 @@
             g_y = rcopy(mine, mine, gw_s.at[2], gw_r.at[2], dev(z, 1 - y, c))
             g_y.start()
 
-        if t == min(1, n_z - 2):
-            theirs = gw_ref.at[g_row(rep, c), g_col(1 - y)]
-            rcopy(theirs, theirs, gw_s.at[2], gw_r.at[2], dev(z, 1 - y, c)).wait_recv()
-            strip = gw_ref.at[g_row(rep, c)]
-            g_c = rcopy(strip, strip, gw_s.at[3], gw_r.at[3], dev(z, y, 1 - c))
-            g_c.start()
-    ya = rcopy(part.at[z, 1 - y, c, ROWS_A], rya, rs_s.at[2, 0, 0], rs_r.at[2, 0, 0], dev(z, 1 - y, c))
-    ya.start()
+    take_all(take_b, zb_copy, n_z - 2)
+    xo[rep, ROWS_B] = part[z, y, c, ROWS_B]
+    for j in range(1, n_rep):
+        xo_copy(j, ROWS_B, 1).start()
+    theirs = gw_ref.at[g_row(rep, c), g_col(1 - y)]
+    rcopy(theirs, theirs, gw_s.at[2], gw_r.at[2], dev(z, 1 - y, c)).wait_recv()
+    strip = gw_ref.at[g_row(rep, c)]
+    g_c = rcopy(strip, strip, gw_s.at[3], gw_r.at[3], dev(z, y, 1 - c))
+    g_c.start()
 
     strip2 = gw_ref.at[g_row(rep, 1 - c)]
     rcopy(strip2, strip2, gw_s.at[3], gw_r.at[3], dev(z, y, 1 - c)).wait_recv()
@@ -383,13 +429,13 @@
     for j in range(1, n_rep):
         gx_copy(j).start()
     ya.wait_recv()
-    xo[rep, ROWS_B] = part[z, y, c, ROWS_B]
     xo[rep, ROWS_A] = (part[z, y, c, ROWS_A].astype(F32) + rya[...].astype(F32)).astype(BF16)
     for j in range(1, n_rep):
-        x_copy(xo, 1, j).start()
-
-    for j in range(1, n_rep):
-        x_copy(xo, 1, j, True).wait_recv()
+        xo_copy(j, ROWS_A, 2).start()
+
+    for j in range(1, n_rep):
+        xo_copy(j, ROWS_B, 1, True).wait_recv()
+        xo_copy(j, ROWS_A, 2, True).wait_recv()
     out = back_ref[...].astype(F32)
     for r in range(n_rep):
         out = out + xo[r].astype(F32)
@@ -411,13 +457,18 @@
                 pl.when(recv_ok(d, t))(sib(kind, origin(d, t), 1 + 2 * t + d).wait_send)
             pl.when(rs_send_ok2(d, t))(za_copy(d, t).wait_send)
             pl.when(rs_send_ok2(d, t))(zb_copy(d, t).wait_send)
+    if short:
+        for d in range(2):
+            pl.when(jump_ok(d))(a_z(d, 1, True).wait_send)
+            pl.when(jump_ok(d))(b_z(d, 1, True).wait_send)
     for d in range(n_z):
         rc_copy(d).wait_send()
         yb_copy(d).wait_send()
     ya.wait_send()
     for j in range(1, n_rep):
         x_copy(xg, 0, j).wait_send()
-        x_copy(xo, 1, j).wait_send()
+        xo_copy(j, ROWS_B, 1).wait_send()
+        xo_copy(j, ROWS_A, 2).wait_send()
         gx_copy(j).wait_send()
     for j in range(1, n_z):
         gz_copy(j).wait_send()
@@ -440,7 +491,7 @@
     hid = weight.shape[1]
     n_c, n_y = 2, 2
     n_z = n_grp // (n_c * n_y)
-    half = rows // 2
+    cut = rows // 4
     vmem = pl.BlockSpec(memory_space=pltpu.VMEM)
     dma = pltpu.SemaphoreType.DMA
     g_rows = width // (n_rep * n_c)
@@ -466,10 +517,10 @@
             pltpu.VMEM((n_z, n_y, n_c, rows, width), BF16),
             pltpu.VMEM((n_z, n_y, n_c, rows, width), BF16),
             pltpu.VMEM((n_z, n_y, rows, width), BF16),
-            pltpu.VMEM((2, n_z - 1, n_y, half, width), BF16),
-            pltpu.VMEM((2, n_z - 1, half, width), BF16),
-            pltpu.VMEM((half, width), BF16),
-            pltpu.VMEM((n_z, half, width), BF16),
+            pltpu.VMEM((2, n_z - 1, n_y, cut, width), BF16),
+            pltpu.VMEM((2, n_z - 1, rows - cut, width), BF16),
+            pltpu.VMEM((cut, width), BF16),
+            pltpu.VMEM((n_z, rows - cut, width), BF16),
             pltpu.VMEM((n_rep, rows, width), BF16),
             pltpu.VMEM((n_rep, rows, width), BF16),
             pltpu.VMEM((width, hid), F32),
@@ -482,7 +533,7 @@
             dma((2, 2 * n_z)), dma((2, 2 * n_z)),
             dma((n_z,)), dma((n_z,)),
             dma((4, 2, n_z)), dma((4, 2, n_z)),
-            dma((2, n_rep)), dma((2, n_rep)),
+            dma((3, n_rep)), dma((3, n_rep)),
             dma((4,)), dma((4,)),
             dma((n_z,)), dma((n_z,)),
             dma((n_rep,)), dma((n_rep,)),

time: 67.3 us -> 64.6 us (0.960)
  the two profiles are of different devices: /device:TPU:0 before, /device:TPU:16 now
where the time goes in v3:
time: 64.6 us; the launch traced here: 64.5 us
  Pallas kernels  63.8 us (99%)
    pallas_call x1, Pallas kernels, per_device(): pl.pallas_call(functools.partial(main_kernel, n_rep, n_z, n_y, n_c, float...  61.9 us
    pallas_call x1, Pallas kernels, per_device(): pl.pallas_call(finish_kernel, out_shape=tuple((jax.ShapeDtypeStruct(o.sha...  1.94 us

profile of v3, /device:TPU:16, one launch (start us, length us, event | category | flops | bytes accessed | tf_op | source)
XLA Modules:
  0.0 64.5 jit_solution(15835600607385984242)
XLA Ops:
  0.6 61.9 %shard_map.112 = (bf16[512,256]{1,0:T(8,128)(2,1)}, f32[128,256]{1,0:T(8,128)}, f32[512,128]{1,0:T(8,128)}) custom-call(s32[16]{0:T(128)} %owner_ref.1, s32[1,1,8,12]{3,2,1,0:T(8,128)} %row_ref.1, s32[1,1,8,12]{3,2,1,0:T(8,128)} %col_ref.1, s32[1,1,8]{2,1,0:T(1,128)} %count_ref.1, bf16[512,128]{1,0:T(8,128)(2,1)} %feat_hbm.1, bf16[128,256]{1,0:T(8,128)(2,1)} %weight_hbm.1, ...), custom_call_target="tpu_custom_call" | custom-call | tf_op jit(solution)/shard_map/pallas_call | solution.py:501
  62.5 1.9 %shard_map.113 = (bf16[512,256]{1,0:T(8,128)(2,1)}, f32[128,256]{1,0:T(8,128)}, f32[512,128]{1,0:T(8,128)}) custom-call(bf16[512,256]{1,0:T(8,128)(2,1)} %get-tuple-element.6.a, f32[128,256]{1,0:T(8,128)} %get-tuple-element.7.b, f32[512,128]{1,0:T(8,128)} %get-tuple-element.8.c), custom_call_target="tpu_custom_call" | custom-call | tf_op jit(solution)/shard_map/pallas_call | solution.py:545
